TPU v7x, 32 devices: a whole 2x2x4 slice. The times are simulated.
32 devices in a mesh: section: 2 (over x), dp: 16 (over z, y, core).
Axes of the slice: x: 2, y: 2, z: 4, core: 2. Of those that a mesh axis runs over, the one named last changes fastest.
Arguments:
- cells: float32 [32, 24, 19, 512], P('dp'), may hold values from -6 to 6
- missing_mask: int32 [32, 24, 19], P('dp'), may hold values 0 or 1
- missing_embed: float32 [512], replicated, may hold values from -6 to 6
- context_rows: int32 [32], P('dp'), may hold values from 2 to 24
- norm_gains: float32 [2, 3, 512], P('section'), may hold values from 0.25 to 1.75
- attn_in: float32 [2, 2, 512, 1536], P('section'), may hold values from -0.375 to 0.375
- attn_out: float32 [2, 2, 512, 512], P('section'), may hold values from -0.75 to 0.75
- mlp_up: float32 [2, 512, 2048], P('section'), may hold values from -0.25 to 0.25
- mlp_down: float32 [2, 2048, 512], P('section'), may hold values from -0.1875 to 0.1875
- cotangent: float32 [32, 24, 19, 512], P('dp'), may hold values from -6 to 6
Outputs:
- layer_outputs: float32 [2, 32, 24, 19, 512], P('section', 'dp')
- input_grads: float32 [2, 32, 24, 19, 512], P('section', 'dp')
- gain_grads: float32 [2, 3, 512], P('section')
- attn_in_grads: float32 [2, 2, 512, 1536], P('section')
- attn_out_grads: float32 [2, 2, 512, 512], P('section')
- up_grads: float32 [2, 512, 2048], P('section')
- down_grads: float32 [2, 2048, 512], P('section')
- missing_grad: float32 [512], replicated
Inputs may be any that keep to these rules, and one draw needn't show every extreme that they name: Only the first context_rows rows of a table are attended to in column attention; every row attends to them.
All inputs are finite; a program needn't handle non-finite values. No bound on the sum of `missing_mask` on one device may be relied on, other than what follows from the above.
Results may differ from a plain program's by a relative error of at most 0.0003.
Values sent between devices are 32-bit elements; how exact they have to be, the bound alone decides.
A program may use at most 192 MiB of HBM per device.

v0:
```python
import functools
from types import SimpleNamespace

import jax
import jax.numpy as jnp
from jax import lax
from jax.experimental import pallas as pl
from jax.experimental.pallas import tpu as pltpu
from jax.sharding import PartitionSpec as P

HEADS = 4
EPSILON = 1e-05
NEG = -1e30
INV_SQRT2PI = 0.3989422804014327
LOG2E = 1.4426950408889634
LN2 = 0.6931471805599453
ERFC_P = 0.33
ERFC_C = (0.1863578482, 0.1829552331, 0.2012284886, 0.0472047191, 0.4085317677, -0.3511862269, 0.4602596132, -0.1353514118)
VMEM_LIMIT = 62 * 1024 * 1024
SUM_VMEM_LIMIT = 38 * 1024 * 1024
TILE = 512
F32, BF16 = jnp.float32, jnp.bfloat16


def dot(a, b, contract=((1,), (0,))):
    return lax.dot_general(a, b, (contract, ((), ())), preferred_element_type=F32)


def split(v):
    hi = v.astype(BF16)
    return hi, (v - hi.astype(F32)).astype(BF16)


def put(ref, index, v):
    hi, lo = split(v)
    ref[(0, *index)] = hi
    ref[(1, *index)] = lo


def parts(ref, *index):
    return ref[(0, *index)], ref[(1, *index)]


def wide(a, b, ca, cb):
    (ah, al), (bh, bl) = a, b
    if ah.shape[ca] < 512:
        return dot(jnp.concatenate([ah, ah, al], ca), jnp.concatenate([bh, bl, bh], cb), ((ca,), (cb,)))
    rows = ah.shape[1 - ca]
    both = dot(jnp.concatenate([ah, al], 1 - ca), bh, ((ca,), (cb,)))
    return both[:rows] + both[rows:] + dot(ah, bl, ((ca,), (cb,)))


def side(a, b):
    (ah, al), (bh, bl) = a, b
    width = bh.shape[1]
    both = dot(ah, jnp.concatenate([bh, bl], 1))
    return both[:, :width] + both[:, width:] + dot(al, bh)


def normalized(h):
    centred = h - jnp.mean(h, axis=-1, keepdims=True)
    rstd = lax.rsqrt(jnp.mean(centred * centred, axis=-1, keepdims=True) + EPSILON)
    return centred * rstd, rstd


def norm_back(n, rstd, gain, da):
    dn = da * gain
    return rstd * (dn - jnp.mean(dn, axis=-1, keepdims=True) - n * jnp.mean(dn * n, axis=-1, keepdims=True))


def cell_ids(start, count, inner, along):
    shape = (count, 1) if along == 0 else (1, count)
    at = lax.broadcasted_iota(jnp.int32, shape, along) + start
    outer = lax.shift_right_logical(at * ((1 << 20) // inner + 1), 20)
    return outer, at - outer * inner


def up16(n):
    return (n + 15) // 16 * 16


def blocks(outer, inner):
    cells = up16(outer * inner)
    half = up16((outer + 1) // 2 * inner)
    first_keys = min(cells, up16((((half - 1) // inner) + 1) * inner))
    second_keys = ((half // inner) * inner) // 16 * 16
    return ((slice(0, half), slice(0, first_keys)), (slice(half, cells), slice(second_keys, cells)))


def when(cond):
    if isinstance(cond, bool):
        return (lambda action: action()) if cond else (lambda action: None)
    return pl.when(cond)


def over(count, action):
    if count <= 4:
        for i in range(count):
            action(i)
    else:
        pl.loop(0, count)(action)


def staggered(units, *steps):
    state = [None] * len(units)
    for i in range(len(units) + 1):
        if i < len(units):
            state[i] = steps[0](*units[i])
        if i > 0:
            for step in steps[1:]:
                state[i - 1] = step(*units[i - 1], state[i - 1])


def lanes(j, width):
    return pl.ds(pl.multiple_of(j * width, width), width)


def start(src, dst, sem):
    copy = pltpu.make_async_copy(src, dst, sem)
    copy.start()
    return copy


def fill_biases(outer, inner, limit, refs, keys_along):
    for (queries, keys), ref in zip(blocks(outer, inner), refs):
        q_outer, _ = cell_ids(queries.start, queries.stop - queries.start, inner, 1 - keys_along)
        k_outer, k_inner = cell_ids(keys.start, keys.stop - keys.start, inner, keys_along)
        ref[...] = jnp.where((q_outer == k_outer) & (k_inner < limit), 0.0, NEG)


def gelu_parts(z):
    size = jnp.abs(z)
    below = 1.0 + (ERFC_P * 0.7071067811865476) * size
    t = pl.reciprocal(below, approx=True)
    t = t * (2.0 - below * t)
    series = jnp.full_like(t, ERFC_C[-1])
    for c in ERFC_C[-2::-1]:
        series = series * t + c
    bell = jnp.exp(-0.5 * z * z)
    tail = 0.5 * (series * t) * bell
    phi = jnp.where(z >= 0.0, 1.0 - tail, tail)
    return z * phi, phi + z * (INV_SQRT2PI * bell)


SMEM, VMEM, ANY = pltpu.SMEM, pltpu.VMEM, pl.ANY


def f32(*shape):
    return jax.ShapeDtypeStruct(shape, F32)


def b16(*shape):
    return jax.ShapeDtypeStruct(shape, BF16)


def dma(*shape):
    return pltpu.SemaphoreType.DMA(shape)


def remote(src, dst, send, recv, device):
    return pltpu.make_async_remote_copy(
        src_ref=src, dst_ref=dst, send_sem=send, recv_sem=recv, device_id=device, device_id_type=pl.DeviceIdType.MESH
    )


def call(name, body, collective_id, ins, outs, scratch, limit):
    names = [*ins, *outs, *scratch]

    def kernel(*refs):
        body(SimpleNamespace(**dict(zip(names, refs))))

    results = pl.pallas_call(
        kernel,
        out_shape=[t for t, _ in outs.values()],
        in_specs=[pl.BlockSpec(memory_space=s) for _, s in ins.values()],
        out_specs=[pl.BlockSpec(memory_space=s) for _, s in outs.values()],
        scratch_shapes=list(scratch.values()),
        compiler_params=pltpu.CompilerParams(
            vmem_limit_bytes=limit, collective_id=collective_id, has_side_effects=collective_id is not None
        ),
        name=name,
    )(*(a for a, _ in ins.values()))
    return dict(zip(outs, results))


class Layers:
    SPLIT_ROWS = 64

    def __init__(self, tables, rows, feat, width, ff):
        self.tables, self.rows, self.feat, self.width, self.ff = tables, rows, feat, width, ff
        self.real, self.cells = rows * feat, up16(rows * feat)
        self.hd = width // HEADS
        self.scale = self.hd ** (-0.5)

    def sites(self, r, site, keys_along):
        if site == 1:
            ranges, biases = blocks(self.feat, self.rows), r.col_bias
        else:
            ranges, biases = blocks(self.rows, self.feat), r.row_bias
        return [(*unit, bias) for unit, bias in zip(ranges, biases[keys_along])]

    def missing(self, r, table):
        mask = r.mask[table]
        return [(slice(f * self.rows, (f + 1) * self.rows), mask[:, f : f + 1] == 1) for f in range(self.feat)]

    def set_out(self, r, src, count):
        for k in range(self.width // 128):
            r.perm_v[k, 0:count] = src[0:count, k * 128 : (k + 1) * 128]

    def by_rows(self, r, dst):
        for row in range(self.rows):
            for k in range(self.width // 128):
                at = (slice(row * self.feat, (row + 1) * self.feat), slice(k * 128, (k + 1) * 128))
                dst[at] = r.perm_v[k, pl.ds(row, self.feat, stride=self.rows), :]

    def by_features(self, r, dst):
        for feat in range(self.feat):
            for k in range(self.width // 128):
                at = (slice(feat * self.rows, (feat + 1) * self.rows), slice(k * 128, (k + 1) * 128))
                dst[at] = r.perm_v[k, pl.ds(feat, self.rows, stride=self.feat), :]

    def __call__(self, cells, mask, embed, context, gains, weights, cotangent):
        t, c, w, ff, real = self.tables, self.cells, self.width, self.ff, self.real
        rows, feat = self.rows, self.feat
        ins = {
            "cells": (cells, ANY),
            "mask": (mask, VMEM),
            "embed": (embed, VMEM),
            "ctx": (context, SMEM),
            "gains": (gains, VMEM),
            "cot": (cotangent, ANY),
        }
        names = ("win", "wout", "wup", "wdown")
        ins |= {n: (a, ANY) for n, a in zip(names, weights)}
        outs = {
            "out": f32(t, real, w),
            "din": f32(t, real, w),
            "ns": f32(t, 3, c, w),
            "qkvs": b16(t, 2, 2, c, 3 * w),
            "gps": f32(t, c, ff),
            "as_": b16(t, 2, 3, c, w),
            "os": b16(t, 2, 2, c, w),
            "gs": b16(t, 2, c, ff),
            "dys": b16(t, 2, c, w),
            "dzs": b16(t, 2, c, ff),
            "dhs": b16(t, 2, 2, c, w),
            "dqkvs": b16(t, 2, 2, c, 3 * w),
        }
        outs = {n: (s, ANY) for n, s in outs.items()} | {"small": (f32(8, w), VMEM)}
        scratch = {n + "_v": VMEM((2, *a.shape), BF16) for n, a in zip(names, weights)}
        scratch |= {
            "h_v": VMEM((2, c, w), F32),
            "n_v": VMEM((3, c, w), F32),
            "qkv_v": VMEM((2, 2, c, 3 * w), BF16),
            "o_v": VMEM((2, 2, c, w), BF16),
            "gp_v": VMEM((c, ff), F32),
            "g_v": VMEM((2, c, ff), BF16),
            "a_v": VMEM((2, 3, c, w), BF16),
            "y_v": VMEM((t, c, w), F32),
            "dqkv_f": VMEM((c, 3 * w), F32),
            "perm_v": VMEM((w // 128, c, 128), F32),
            "dys_v": VMEM((2, c, w), BF16),
            "dy_v": VMEM((c, w), F32),
            "do_v": VMEM((2, c, w), BF16),
            "got": VMEM((t, real, w), F32),
            "stat_v": VMEM((t, c, 128), F32),
            "lse_v": VMEM((t, 2 * HEADS, c), F32),
            "spare_v": VMEM((w // 2, w), F32),
            "raw_sem": pltpu.SemaphoreType.DMA((20,)),
            "in_sem": pltpu.SemaphoreType.DMA((4,)),
            "out_sem": pltpu.SemaphoreType.DMA((18,)),
            "send": pltpu.SemaphoreType.DMA((t, 2)),
            "recv": pltpu.SemaphoreType.DMA((t, 2)),
        }
        for name, ranges in (("col_bias", blocks(feat, rows)), ("row_bias", blocks(rows, feat))):
            for i, (queries, keys) in enumerate(ranges):
                shape = (queries.stop - queries.start, keys.stop - keys.start)
                scratch[f"{name}0{i}"] = VMEM(shape[::-1], F32)
                scratch[f"{name}1{i}"] = VMEM(shape, F32)

        def body(r):
            for n in ("col_bias", "row_bias"):
                setattr(r, n, [[getattr(r, f"{n}{along}{i}") for i in range(2)] for along in range(2)])
            self.kernel(r)

        return call("layers", body, 1, ins, outs, scratch, VMEM_LIMIT)

    def raw_pieces(self, r):
        w, ff = self.width, self.ff
        half, wide_in, step = w // 2, 3 * w, self.SPLIT_ROWS
        top, rest, whole = slice(0, half), slice(half, w), slice(None)
        big, bigger = r.dqkv_f.at[top], r.gp_v.at[top]
        pieces = [
            (r.win.at[0, top], big, r.win_v, (0,), 0, whole, 0),
            (r.win.at[0, rest], bigger.at[:, 0:wide_in], r.win_v, (0,), half, whole, 1),
            (r.wout.at[0, top], r.h_v.at[0, top], r.wout_v, (0,), 0, whole, 2),
            (r.wout.at[0, rest], r.h_v.at[1, top], r.wout_v, (0,), half, whole, 3),
            (r.win.at[1, top], big, r.win_v, (1,), 0, whole, 0),
            (r.win.at[1, rest], bigger.at[:, 0:wide_in], r.win_v, (1,), half, whole, 1),
            (r.wout.at[1, top], r.n_v.at[0, top], r.wout_v, (1,), 0, whole, 4),
            (r.wout.at[1, rest], r.spare_v, r.wout_v, (1,), half, whole, 5),
        ]
        self.attention_pieces = len(pieces)
        pieces.append((r.wup.at[top], bigger, r.wup_v, (), 0, whole, 1))
        pieces.append((r.wup.at[rest, 0:wide_in], big, r.wup_v, (), half, slice(0, wide_in), 0))
        pieces.append((r.wup.at[rest, wide_in:ff], r.spare_v, r.wup_v, (), half, slice(wide_in, ff), 5))
        high = self.cells // step * step
        buffers = [r.y_v.at[0, 0:high], r.y_v.at[1, 0:high]]
        low = slice(half, half + (self.cells - half) // step * step)
        for k in range(3):
            buffers.append(r.dqkv_f.at[low, k * w : (k + 1) * w])
        for k in range(ff // w):
            buffers.append(r.gp_v.at[low, k * w : (k + 1) * w])
        at = 0
        for i, buffer in enumerate(buffers):
            size = min(buffer.shape[0], ff - at)
            if size:
                pieces.append((r.wdown.at[at : at + size], buffer.at[0:size], r.wdown_v, (), at, whole, 6 + i))
            at += size
        assert at == ff
        return pieces

    def raw_copy(self, r, i):
        src, buffer = self.raw_pieces(r)[i][:2]
        return pltpu.make_async_copy(src, buffer, r.raw_sem.at[i])

    def split_piece(self, r, i):
        pieces = self.raw_pieces(r)
        _, buffer, v, lead, at, columns, user = pieces[i]
        step = self.SPLIT_ROWS
        self.raw_copy(r, i).wait()

        @pl.loop(0, buffer.shape[0] // step)
        def _(j):
            src = pl.ds(pl.multiple_of(j * step, step), step)
            dst = pl.ds(pl.multiple_of(at + j * step, step), step)
            put(v, (*lead, dst, columns), buffer[src])

        later = [k for k in range(i + 1, len(pieces)) if pieces[k][-1] == user]
        if later:
            self.raw_copy(r, later[0]).start()

    def start_raw(self, r):
        seen = set()
        for i, piece in enumerate(self.raw_pieces(r)):
            if piece[-1] not in seen:
                self.raw_copy(r, i).start()
            seen.add(piece[-1])

    def split_attention(self, r):
        for i in range(self.attention_pieces):
            self.split_piece(r, i)

    def split_mlp(self, r):
        for i in range(self.attention_pieces, len(self.raw_pieces(r))):
            self.split_piece(r, i)

    def kernel(self, r):
        t, real, c = self.tables, self.real, self.cells
        section = lax.axis_index("section")
        other = {"section": 1 - section}
        barrier = pltpu.get_barrier_semaphore()
        pl.semaphore_signal(barrier, inc=1, device_id=other, device_id_type=pl.DeviceIdType.MESH)
        self.start_raw(r)

        @pl.when(section == 0)
        def _():
            start(r.cells.at[0], r.dy_v.at[0:real], r.in_sem.at[0])

        self.split_attention(r)

        @pl.when(section == 1)
        def _():
            self.split_mlp(r)

        for along in range(2):
            fill_biases(self.rows, self.feat, self.feat, r.row_bias[along], along)
        r.small[...] = jnp.zeros_like(r.small)
        pl.semaphore_wait(barrier, 1)

        def relay(table, half):
            at = slice(half * self.width // 2, (half + 1) * self.width // 2)
            src, dst = r.y_v.at[table, 0:real, at], r.got.at[table, :, at]
            return remote(src, dst, r.send.at[table, half], r.recv.at[table, half], other)

        @pl.loop(0, 2 * t)
        def _(step):
            forward = (1 - section) * (1 - step // t) + section * (1 - step % 2)
            table = (1 - section) * (step % t) + section * (step // 2)

            @pl.when(forward == 1)
            def _():
                self.forward(r, table, section, relay, step)

            @pl.when(forward == 0)
            def _():
                self.backward(r, table, section, relay)

        @pl.when(section == 1)
        def _():
            for table in range(t):
                for half in range(2):
                    relay(table, half).wait_send()

    def forward(self, r, table, section, relay, step):
        c, w, ff, hd, real = self.cells, self.width, self.ff, self.hd, self.real
        stores, held = [], []

        def keep(src, dst, to_reload=False):
            copy = pltpu.make_async_copy(src, dst, r.out_sem.at[len(stores) + len(held)])
            if to_reload:
                held.append(copy)
                pl.when(section == 0)(copy.start)
            else:
                stores.append(copy)
                copy.start()

        for level in range(2):
            r.h_v[level, real:, :] = jnp.zeros((c - real, w), F32)

        def keep_column(k, at, value):
            column = lax.broadcasted_iota(jnp.int32, (1, r.stat_v.shape[2]), 1) == k
            r.stat_v[table, at, :] = jnp.where(column, value, r.stat_v[table, at, :])

        def norm(site):
            n, rstd = normalized(r.h_v[site % 2])
            r.n_v[site] = n
            keep(r.n_v.at[site], r.ns.at[table, site], True)
            keep_column(2 * HEADS + site, slice(None), rstd)
            put(r.a_v, (site,), n * r.gains[site])
            keep(r.a_v.at[:, site], r.as_.at[table, :, site])

        fill_biases(self.feat, self.rows, r.ctx[table], r.col_bias[1], 1)

        @pl.when(section == 0)
        def _():
            load = pltpu.make_async_copy(r.cells.at[table], r.dy_v.at[0:real], r.in_sem.at[0])
            pl.when(step > 0)(load.start)
            load.wait()
            for at, missing in self.missing(r, table):
                r.dy_v[at] = jnp.where(missing, r.embed[...], r.dy_v[at])
            self.set_out(r, r.dy_v, real)

        @pl.when(section == 1)
        def _():
            start(r.cot.at[table], r.dy_v.at[0:real], r.in_sem.at[1])
            for half in range(2):
                relay(table, half).wait_recv()
            self.set_out(r, r.got.at[table], real)

        self.by_rows(r, r.h_v.at[0])
        for site in range(2):
            norm(site)

            def project(j):
                at = slice(j * TILE, (j + 1) * TILE)
                return wide(parts(r.a_v, site), parts(r.win_v, site, slice(None), at), 1, 0)

            def keep_projected(j, out):
                if j < w // TILE:
                    out = out * (self.scale * LOG2E)
                put(r.qkv_v, (site, slice(None), slice(j * TILE, (j + 1) * TILE)), out)

            staggered([(j,) for j in range(3 * w // TILE)], project, keep_projected)
            keep(r.qkv_v.at[:, site], r.qkvs.at[table, :, site], True)

            def scores(head, queries, keys, bias):
                q = parts(r.qkv_v, site, queries, lanes(head, hd))
                k = parts(r.qkv_v, site, keys, lanes(HEADS + head, hd))
                return wide(q, k, 1, 1)

            def softmax(head, queries, keys, bias, s):
                s = s + bias[...]
                top = jnp.max(s, axis=-1, keepdims=True)
                e = jnp.exp2(s - top)
                total = jnp.sum(e, axis=-1, keepdims=True)
                keep_column(site * HEADS + head, queries, top + jnp.log2(total))
                return split(e), 1.0 / total

            def blend(head, queries, keys, bias, state):
                e, inverse = state
                v = parts(r.qkv_v, site, keys, lanes(2 * HEADS + head, hd))
                put(r.o_v, (site, queries, lanes(head, hd)), side(e, v) * inverse)

            @pl.loop(0, HEADS // 2)
            def _(two):
                units = [(head, *unit) for head in (2 * two, 2 * two + 1) for unit in self.sites(r, site, 1)]
                staggered(units, scores, softmax, blend)

            keep(r.o_v.at[:, site], r.os.at[table, :, site])
            after = r.h_v[site] + wide(parts(r.o_v, site), parts(r.wout_v, site), 1, 0)
            if site == 0:
                self.set_out(r, after, c)
                self.by_features(r, r.h_v.at[1])
            else:
                r.h_v[0] = after
        r.lse_v[table] = r.stat_v[table].T[0 : 2 * HEADS]
        norm(2)

        @pl.when((section == 0) & (step == 0))
        def _():
            self.split_mlp(r)

        def up(j):
            return wide(parts(r.a_v, 2), parts(r.wup_v, slice(None), slice(j * TILE, (j + 1) * TILE)), 1, 0)

        tiles = ff // TILE
        z = up(0)
        for j in range(tiles):
            at = slice(j * TILE, (j + 1) * TILE)
            following = up(j + 1) if j + 1 < tiles else None
            g, gp = gelu_parts(z)
            put(r.g_v, (slice(None), at), g)
            r.gp_v[:, at] = gp
            z = following
        keep(r.g_v, r.gs.at[table])
        keep(r.gp_v, r.gps.at[table], True)
        for half in range(2):
            at = slice(half * w // 2, (half + 1) * w // 2)
            r.y_v[table, :, at] = r.h_v[0, :, at] + wide(parts(r.g_v), parts(r.wdown_v, slice(None), at), 1, 0)

            @pl.when(section == 0)
            def _():
                relay(table, half).start()

        keep(r.y_v.at[table, 0:real], r.out.at[table])
        for copy in stores:
            copy.wait()

        @pl.when(section == 0)
        def _():
            for copy in held:
                copy.wait()

    def backward(self, r, table, section, relay):
        c, w, ff, hd, real = self.cells, self.width, self.ff, self.hd, self.real
        stores = []

        def keep(src, dst):
            stores.append(start(src, dst, r.out_sem.at[len(stores)]))

        fill_biases(self.feat, self.rows, r.ctx[table], r.col_bias[0], 0)

        @pl.when(section == 0)
        def _():
            loads = [
                start(r.ns.at[table], r.n_v, r.in_sem.at[0]),
                start(r.qkvs.at[table], r.qkv_v, r.in_sem.at[1]),
                start(r.gps.at[table], r.gp_v, r.in_sem.at[2]),
            ]
            for half in range(2):
                relay(table, half).wait()
            r.dy_v[0:real] = r.got[table]
            for copy in loads:
                copy.wait()

        @pl.when(section == 1)
        def _():
            pltpu.make_async_copy(r.cot.at[table], r.dy_v.at[0:real], r.in_sem.at[1]).wait()

        r.dy_v[real:, :] = jnp.zeros((c - real, w), F32)
        put(r.dys_v, (), r.dy_v[...])
        keep(r.dys_v, r.dys.at[table])

        def down(j):
            return wide(parts(r.dys_v), parts(r.wdown_v, slice(j * TILE, (j + 1) * TILE)), 1, 1)

        tiles = ff // TILE
        dg = down(0)
        for j in range(tiles):
            at = slice(j * TILE, (j + 1) * TILE)
            following = down(j + 1) if j + 1 < tiles else None
            put(r.g_v, (slice(None), at), dg * r.gp_v[:, at])
            dg = following
        keep(r.g_v, r.dzs.at[table])
        da = wide(parts(r.g_v), parts(r.wup_v), 1, 1)

        def through_norm(site, da):
            n, k = r.n_v[site], 2 * HEADS + site
            rstd = r.stat_v[table, :, k : k + 1]
            r.small[site : site + 1, :] += jnp.sum(da * n, axis=0, keepdims=True)
            return norm_back(n, rstd, r.gains[site], da)

        r.dy_v[...] += through_norm(2, da)
        for site in (1, 0):
            if site == 0:
                self.set_out(r, r.dy_v, real)
                self.by_rows(r, r.dy_v)
            put(r.o_v, (site,), r.dy_v[...])
            keep(r.o_v.at[:, site], r.dhs.at[table, :, site])
            put(r.do_v, (), wide(parts(r.o_v, site), parts(r.wout_v, site), 1, 1))

            def part_of(which, head, span):
                return parts(r.qkv_v, site, span, lanes(which * HEADS + head, hd))

            def products(head, queries, keys, bias):
                do = parts(r.do_v, queries, lanes(head, hd))
                s = wide(part_of(1, head, keys), part_of(0, head, queries), 1, 1)
                return s, wide(part_of(2, head, keys), do, 1, 1)

            def gradients(head, queries, keys, bias, state):
                s, dp = state
                p = jnp.exp2(s + bias[...] - r.lse_v[table, pl.ds(site * HEADS + head, 1), queries])
                ds = p * (dp - jnp.sum(p * dp, axis=0, keepdims=True))
                return split(p), split(ds)

            def back(head, queries, keys, bias, state):
                p, ds = state
                k = part_of(1, head, keys)
                r.dqkv_f[queries, lanes(head, hd)] = (wide(tuple(x.T for x in k), ds, 1, 0) * self.scale).T
                dk = side(ds, part_of(0, head, queries)) * LN2
                dv = side(p, parts(r.do_v, queries, lanes(head, hd)))
                for which, term in ((1, dk), (2, dv)):
                    at = lanes(which * HEADS + head, hd)
                    if keys.start == 0:
                        r.dqkv_f[keys, at] = term
                    else:
                        known = overlap - keys.start
                        if known:
                            r.dqkv_f[keys.start : overlap, at] += term[:known]
                        r.dqkv_f[overlap : keys.stop, at] = term[known:]

            overlap = self.sites(r, site, 0)[0][1].stop

            @pl.loop(0, HEADS // 2)
            def _(two):
                units = [(head, *unit) for head in (2 * two, 2 * two + 1) for unit in self.sites(r, site, 0)]
                staggered(units, products, gradients, back)

            for j in range(3 * w // TILE):
                at = slice(j * TILE, (j + 1) * TILE)
                put(r.qkv_v, (site, slice(None), at), r.dqkv_f[:, at])
            keep(r.qkv_v.at[:, site], r.dqkvs.at[table, :, site])
            da = wide(parts(r.qkv_v, site), parts(r.win_v, site), 1, 1)
            r.dy_v[...] += through_norm(site, da)

        self.set_out(r, r.dy_v, real)
        self.by_features(r, r.dy_v)

        @pl.when(section == 0)
        def _():
            total = jnp.zeros((1, w), F32)
            for at, missing in self.missing(r, table):
                total += jnp.sum(jnp.where(missing, r.dy_v[at], 0.0), axis=0, keepdims=True)
                r.y_v[table, at] = jnp.where(missing, 0.0, r.dy_v[at])
            r.small[3:4, :] += total

        @pl.when(section == 1)
        def _():
            r.y_v[table] = r.dy_v[...]
            for half in range(2):
                relay(table, half).start()

        keep(r.y_v.at[table, 0:real], r.din.at[table])
        for copy in stores:
            copy.wait()


class GradSum:
    ROWS, COLS = 512, 256
    PARTS = 2
    SLACK = 2

    def __init__(self, count, tables, cells, width, ff):
        self.count, self.tables, self.cells, self.width = count, tables, cells, width
        self.rest = count // 4
        shapes = [("gs", None, "dys", None, "down", None, ff, width), ("as_", 2, "dzs", None, "up", None, width, ff)]
        for site in (1, 0):
            shapes.append(("as_", site, "dqkvs", site, "win", site, width, 3 * width))
            shapes.append(("os", site, "dhs", site, "wout", site, width, width))
        self.groups, at = [], 0
        for *which, k, n in shapes:
            blocks = (k // self.ROWS) * (n // self.COLS)
            self.groups.append((at, at + blocks, *which, n // self.COLS))
            at += blocks
        self.blocks = at
        self.chunks = self.blocks * self.PARTS
        self.hops = self.rest // 2 - 1
        self.sends = self.SLACK * (self.hops + 1) + 2
        self.rows = self.ROWS // self.PARTS
        self.ring = self.SLACK // self.PARTS + 2
        self.depth = (cells + 127) // 128 * 128

    def select(self, q, action):
        for group in self.groups:
            first, stop, *_, across = group

            @pl.when((q >= first) & (q < stop))
            def _():
                action(group, (q - first) // across, (q - first) % across)

    def starts_row(self, q):
        found = False
        for first, stop, *_, across in self.groups:
            found = found | ((q >= first) & (q < stop) & ((q - first) % across == 0))
        return found

    def load(self, r, q):
        slot = q % 2

        def action(group, i, j):
            _, _, left, left_site, right, right_site, *_ = group
            a, b = getattr(r, left), getattr(r, right)

            def at(t, part, site):
                return (t, part, slice(None)) if site is None else (t, part, site, slice(None))

            for t in range(self.tables):
                rows = slice(t * self.depth, t * self.depth + self.cells)
                for part in range(2):
                    sem = 2 * t + part
                    start(b.at[(*at(t, part, right_site), lanes(j, self.COLS))], r.b_v.at[slot, part, rows], r.b_sem.at[slot, sem])

                    @pl.when(j == 0)
                    def _():
                        start(a.at[(*at(t, part, left_site), lanes(i, self.ROWS))], r.a_v.at[part, rows], r.a_sem.at[sem])

        self.select(q, action)

    def each_operand(self):
        return [(2 * t + part, part, slice(t * self.depth, t * self.depth + self.cells)) for t in range(self.tables) for part in range(2)]

    def product(self, r, q):
        slot = q % 2

        @pl.when(self.starts_row(q))
        def _():
            for sem, part, rows in self.each_operand():
                a = r.a_v.at[part, rows]
                pltpu.make_async_copy(a, a, r.a_sem.at[sem]).wait()
            for part in range(2):
                r.left_v[part] = r.a_v[part].T

        for sem, part, rows in self.each_operand():
            b = r.b_v.at[slot, part, rows]
            pltpu.make_async_copy(b, b, r.b_sem.at[slot, sem]).wait()

        @pl.when(q + 1 < self.blocks)
        def _():
            self.load(r, q + 1)

        r.products[q % self.ring] = side(parts(r.left_v), parts(r.b_v.at[slot]))

    def kernel(self, r):
        rest, rows, ring = self.rest, self.rows, self.ring
        half = rows // 2
        quart = half // 2
        me, section = lax.axis_index("dp"), lax.axis_index("section")
        core, pair, place = me % 2, me // 2 % 2, me // 4
        sibling, neighbour = {"dp": me + 1 - 2 * core}, {"dp": me + 2 - 4 * pair}
        far = place // (rest // 2)
        along = (1 - far) * place + far * (rest - 1 - place)
        inward, outward = {"dp": me + 4 - 8 * far}, {"dp": me - 4 + 8 * far}
        hops = self.hops

        def peer(j):
            return {"dp": lax.rem(place + j, rest) * 4 + me % 4}

        def span(at, size):
            return pl.ds(pl.multiple_of(at, size), size)

        mine = core * half
        own, other = pair * quart, (1 - pair) * quart
        keeps, gives = far * quart, (1 - far) * quart

        barrier = pltpu.get_barrier_semaphore()

        def greet(device):
            pl.semaphore_signal(barrier, inc=1, device_id=device, device_id_type=pl.DeviceIdType.MESH)

        greet(sibling)
        greet(neighbour)

        @pl.loop(1, rest)
        def _(j):
            greet(peer(j))

        for t in range(self.tables):
            pad = slice(t * self.depth + self.cells, (t + 1) * self.depth)
            for part in range(2):
                r.a_v[part, pad] = jnp.zeros_like(r.a_v[part, pad])
                for slot in range(2):
                    r.b_v[slot, part, pad] = jnp.zeros_like(r.b_v[slot, part, pad])
        self.load(r, 0)
        passing = [
            start(getattr(r, f"table{i}"), getattr(r, f"out{i}"), r.table_sem.at[i]) for i in range(self.passed)
        ]

        @pl.when(section == 1)
        def _():
            greet({"section": 0})

        pl.semaphore_wait(barrier, rest + 2 - section)

        def copy(which, c, src, dst, device):
            return remote(src, dst, r.send.at[which, c % self.sends], r.recv.at[which, c], device)

        def product_rows(c, which):
            return c // self.PARTS % ring, span(c % self.PARTS * rows + which * half, half)

        def halve(c):
            return copy(0, c, r.products.at[product_rows(c, 1 - core)], r.sums.at[c], sibling)

        def gather_half(c):
            at = r.full.at[c, span(mine, half)]
            return copy(1, c, at, at, sibling)

        def quarter(c):
            return copy(2, c, r.sums.at[c, span(other, quart)], r.got_near.at[c], neighbour)

        def gather_quarter(c):
            at = r.full.at[c, span(mine + own, quart)]
            return copy(3, c, at, at, neighbour)

        def add_up(c):
            return copy(2, c, r.sums.at[c, span(keeps, quart)], r.got_near.at[c], neighbour)

        def come(kind, c):
            if kind == 0:
                return copy(4, c, r.sums.at[c, span(own, quart)], r.got_in.at[c, 0:quart], inward)
            return copy(4, c, r.sums.at[c], r.got_in.at[c], inward)

        def meet(kind, c):
            at = span(own if kind == 0 else gives, quart)
            return copy(5, c, r.sums.at[c, at], r.got_mid.at[c], inward)

        def give_back(c):
            at = r.full.at[c, span(mine + keeps, quart)]
            return copy(6, c, at, at, inward)

        def leave(kind, c):
            at = r.full.at[c, span(mine + own, quart) if kind == 0 else span(mine, half)]
            return copy(7, c, at, at, outward)

        def reduced(kind, c, h, at_end):
            @pl.when((along == h) & (h < hops))
            def _():
                come(kind, c).start()

            @pl.when((along == h) & (h == hops))
            def _():
                at_end(c)

        def come_hop(kind, c, h):
            @pl.when(along == h)
            def _():
                come(kind, c).wait_send()

            @pl.when(along == h + 1)
            def _():
                come(kind, c).wait_recv()
                if kind == 0:
                    r.sums[c, span(own, quart)] += r.got_in[c, 0:quart]
                else:
                    r.sums[c] += r.got_in[c]

            reduced(kind, c, h + 1, lambda c: meet(kind, c).start())

        def pass_out(kind, c, h):
            @pl.when((along == h) & (h > 0))
            def _():
                leave(kind, c).start()

            if kind == 0:

                @pl.when(along == h)
                def _():
                    gather_quarter(c).start()

        def leave_hop(kind, c, g):
            h = hops - g

            @pl.when(along == h)
            def _():
                leave(kind, c).wait_send()

            @pl.when(along == h - 1)
            def _():
                leave(kind, c).wait_recv()

            pass_out(kind, c, h - 1)

        def after_halve(c):
            halve(c).wait()
            r.sums[c] += r.products[product_rows(c, core)]

            @pl.when(core == 0)
            def _():
                quarter(c).start()

            @pl.when(core == 1)
            def _():
                reduced(1, c, 0, lambda c: meet(1, c).start())

        def after_quarter(c):
            quarter(c).wait()
            r.sums[c, span(own, quart)] += r.got_near[c]
            reduced(0, c, 0, lambda c: meet(0, c).start())

        def after_meet(kind, c):
            @pl.when(along == hops)
            def _():
                meet(kind, c).wait()
                if kind == 0:
                    r.full[c, span(mine + own, quart)] = r.sums[c, span(own, quart)] + r.got_mid[c]
                else:
                    r.sums[c, span(keeps, quart)] += r.got_mid[c]
                    add_up(c).start()

            if kind == 0:
                pass_out(0, c, hops)

        def after_add_up(c):
            @pl.when(along == hops)
            def _():
                add_up(c).wait()
                r.full[c, span(mine + keeps, quart)] = r.sums[c, span(keeps, quart)] + r.got_near[c]
                give_back(c).start()

        def after_give_back(c):
            @pl.when(along == hops)
            def _():
                give_back(c).wait()

            pass_out(1, c, hops)

        def gathered(c):
            @pl.when(core == 0)
            def _():
                gather_quarter(c).wait()

            gather_half(c).start()

        def after_gather_half(c):
            gather_half(c).wait()

        def small_copy(k, device):
            return remote(r.small_v.at[k], r.got_small.at[k], r.small_send.at[k], r.small_recv.at[k], device)

        def small_rest(j):
            dst = r.got_small.at[2 + j]
            return remote(r.small_v.at[3], dst, r.small_send.at[2 + j], r.small_recv.at[2 + j], peer(j))

        def small_step(step):
            @pl.when(step == 2)
            def _():
                r.small_v[1] = r.small[...]
                small_copy(1, sibling).start()

            @pl.when(step == 4)
            def _():
                small_copy(1, sibling).wait()
                r.small_v[2] = r.small_v[1] + r.got_small[1]
                small_copy(2, neighbour).start()

            @pl.when(step == 6)
            def _():
                small_copy(2, neighbour).wait()
                r.small_v[3] = r.small_v[2] + r.got_small[2]
                pl.loop(1, rest)(lambda j: small_rest(j).start())

            @pl.when(step == 8)
            def _():
                pl.loop(1, rest)(lambda j: small_rest(j).wait())
                total = r.small_v[3]
                for j in range(1, rest):
                    total += r.got_small[2 + j]
                r.small_v[0] = total

                @pl.when(section == 0)
                def _():
                    small_copy(0, {"section": 1}).start()

        last = 2 * hops + 5

        def delay(time):
            return self.SLACK * time - (1 if time < last else 2)

        @pl.loop(0, self.chunks + delay(last))
        def _(step):
            def stage(time, action):
                c = step - (delay(time) if isinstance(time, int) else self.SLACK * time - 1)

                @pl.when((c >= 0) & (c < self.chunks))
                def _():
                    action(c)

            stage(last, after_gather_half)

            @pl.when(core == 0)
            def _():
                over(hops, lambda g: stage(hops + 4 + g, lambda c: leave_hop(0, c, g)))
                stage(hops + 3, lambda c: after_meet(0, c))
                over(hops, lambda h: stage(3 + h, lambda c: come_hop(0, c, h)))
                stage(2, after_quarter)

            @pl.when(core == 1)
            def _():
                over(hops, lambda g: stage(hops + 5 + g, lambda c: leave_hop(1, c, g)))
                stage(hops + 4, after_give_back)
                stage(hops + 3, after_add_up)
                stage(hops + 2, lambda c: after_meet(1, c))
                over(hops, lambda h: stage(2 + h, lambda c: come_hop(1, c, h)))

            stage(last - 1, gathered)
            stage(1, after_halve)
            small_step(step)

            @pl.when(step < self.chunks)
            def _():
                @pl.when(step % self.PARTS == 0)
                def _():
                    self.product(r, step // self.PARTS)

                halve(step).start()

        for load in passing:
            load.wait()
        r.small_out[...] = r.small_v[0]

        @pl.when(section == 0)
        def _():
            small_copy(0, {"section": 1}).wait_send()

        @pl.when(section == 1)
        def _():
            small_copy(0, {"section": 1}).wait_recv()
            r.small_out[3:4] = r.got_small[0, 3:4]

    def __call__(self, operands, small, tables):
        t, width, deep = self.tables, self.width, self.tables * self.depth
        rest, chunks, rows, ring, cols = self.rest, self.chunks, self.rows, self.ring, self.COLS
        outs = {"full": VMEM((chunks, rows, cols), F32), "small_out": f32(8, width)}
        outs |= {f"out{i}": VMEM(a.shape, F32) for i, a in enumerate(tables)}
        scratch = {
            "products": VMEM((ring, self.ROWS, cols), F32),
            "sums": VMEM((chunks, rows // 2, cols), F32),
            "got_near": VMEM((chunks, rows // 4, cols), F32),
            "got_mid": VMEM((chunks, rows // 4, cols), F32),
            "got_in": VMEM((chunks, rows // 2, cols), F32),
            "a_v": VMEM((2, deep, self.ROWS), BF16),
            "left_v": VMEM((2, self.ROWS, deep), BF16),
            "b_v": VMEM((2, 2, deep, cols), BF16),
            "small_v": VMEM((4, 8, width), F32),
            "got_small": VMEM((2 + rest, 8, width), F32),
            "a_sem": dma(2 * t),
            "b_sem": dma(2, 2 * t),
            "send": dma(8, self.sends),
            "recv": dma(8, chunks),
            "small_send": dma(2 + rest),
            "small_recv": dma(2 + rest),
        }
        ins = {n: (a, ANY) for n, a in operands.items()} | {"small": (small, VMEM)}
        ins |= {f"table{i}": (a, ANY) for i, a in enumerate(tables)}
        scratch["table_sem"] = dma(len(tables))
        self.passed = len(tables)
        outs = {n: (s, VMEM) for n, s in outs.items()}
        return call("weight_gradient_sum", self.kernel, 0, ins, outs, scratch, SUM_VMEM_LIMIT)

    def results(self, sums, small, tables, ff):
        width = self.width

        def here(a):
            return (pltpu.with_memory_space_constraint(a, pltpu.VMEM), VMEM)

        ins = {"full": here(sums), "small": (small, VMEM)} | {f"table{i}": here(a) for i, a in enumerate(tables)}
        outs = {
            "win": f32(2, width, 3 * width),
            "wout": f32(2, width, width),
            "up": f32(width, ff),
            "down": f32(ff, width),
        } | {f"out{i}": f32(*a.shape) for i, a in enumerate(tables)}
        outs = {n: (s, ANY) for n, s in outs.items()}
        outs |= {"gain": (f32(3, 1, width), VMEM), "missing": (f32(1, width), VMEM)}
        scratch = {"sem": dma(self.chunks), "out_sem": dma(len(tables))}

        def body(r):
            stores = [
                start(getattr(r, f"table{i}"), getattr(r, f"out{i}"), r.out_sem.at[i]) for i in range(len(tables))
            ]
            for first, stop, *_, out, site, across in self.groups:
                dst = getattr(r, out) if site is None else getattr(r, out).at[site]
                for c in range(first * self.PARTS, stop * self.PARTS):
                    q = c // self.PARTS - first
                    row = q // across * self.ROWS + c % self.PARTS * self.rows
                    at = (slice(row, row + self.rows), slice(q % across * self.COLS, (q % across + 1) * self.COLS))
                    stores.append(start(r.full.at[c], dst.at[at], r.sem.at[c]))
            for k in range(3):
                r.gain[k] = r.small[k : k + 1, :]
            r.missing[...] = r.small[3:4, :]
            for copy in stores:
                copy.wait()

        return call("results", body, None, ins, outs, scratch, SUM_VMEM_LIMIT)


def local(
    cells,
    missing_mask,
    missing_embed,
    context_rows,
    norm_gains,
    attn_in,
    attn_out,
    mlp_up,
    mlp_down,
    cotangent,
):
    tables, rows, feat, width = cells.shape
    ff = mlp_up.shape[2]
    layers = Layers(tables, rows, feat, width, ff)

    def flat(tables_of_cells):
        return jnp.swapaxes(tables_of_cells, 1, 2).reshape(tables, rows * feat, -1)

    def unflat(cells_of_tables):
        return jnp.swapaxes(cells_of_tables.reshape(tables, feat, rows, width), 1, 2)[None]

    weights = (attn_in[0], attn_out[0], mlp_up[0], mlp_down[0])
    gains = jnp.swapaxes(norm_gains, 0, 1)
    done = layers(flat(cells), missing_mask, missing_embed[None], context_rows, gains, weights, flat(cotangent))
    operands = {n: done[n] for n in ("as_", "os", "gs", "dys", "dzs", "dhs", "dqkvs")}
    grad_sum = GradSum(lax.axis_size("dp"), tables, layers.cells, width, ff)
    sums = grad_sum(operands, done["small"], (done["out"], done["din"]))
    got = grad_sum.results(sums["full"], sums["small_out"], (sums["out0"], sums["out1"]), ff)
    return (
        unflat(got["out0"]),
        unflat(got["out1"]),
        jnp.swapaxes(got["gain"], 0, 1),
        got["win"][None],
        got["wout"][None],
        got["up"][None],
        got["down"][None],
        got["missing"][0],
    )


def solution(mesh):
    in_specs = (
        P("dp", None, None, None),
        P("dp", None, None),
        P(),
        P("dp"),
        P("section", None, None),
        P("section", None, None, None),
        P("section", None, None, None),
        P("section", None, None),
        P("section", None, None),
        P("dp", None, None, None),
    )
    out_specs = (
        P("section", "dp", None, None, None),
        P("section", "dp", None, None, None),
        P("section", None, None),
        P("section", None, None, None),
        P("section", None, None, None),
        P("section", None, None),
        P("section", None, None),
        P(),
    )
    return jax.shard_map(local, mesh=mesh, in_specs=in_specs, out_specs=out_specs, check_vma=False)
```

profile of v0, /device:TPU:0, one launch (start us, length us, event | category | flops | bytes accessed | tf_op | source)
XLA Modules:
  0.0 376.5 jit_solution(12434186795998128751)
XLA Ops:
  0.6 1.4 copy.18.refs_1_
  2.0 196.3 %layers.1 = (f32[2,456,512]{2,1,0:T(8,128)}, f32[2,456,512]{2,1,0:T(8,128)}, f32[2,3,464,512]{3,2,1,0:T(8,128)}, bf16[2,2,2,464,1536]{4,3,2,1,0:T(8,128)(2,1)}, ...) custom-call(f32[2,456,512]{2,1,0:T(8,128)} %bitcast.32, ...), custom_call_target="tpu_custom_call" | custom-call | tf_op jit(solution)/shard_map/layers/pallas_call | solution.py:172
  198.4 169.1 %weight_gradient_sum.1 = (f32[64,256,256]{2,1,0:T(8,128)S(1)}, f32[8,512]{1,0:T(8,128)}, f32[2,456,512]{2,1,0:T(8,128)S(1)}, f32[2,456,512]{2,1,0:T(8,128)S(1)}) custom-call(bf16[2,2,3,464,512]{4,3,2,1,0:T(8,128)(2,1)} %get-tuple-element.30.refs_0_, bf16[2,2,2,464,512]{4,3,2,1,0:T(8,128)(2,1)} %get-tuple-element.31.refs_1_, ...), custom_call_target="tpu_custom_call" | custom-call | tf_op jit(solution)/shard_map/weight_gradient_sum/pallas_call | solution.py:172
  367.4 8.9 %results.1 = (f32[2,512,1536]{2,1,0:T(8,128)}, f32[2,512,512]{2,1,0:T(8,128)}, f32[512,2048]{1,0:T(8,128)}, f32[2048,512]{1,0:T(8,128)}, f32[2,456,512]{2,1,0:T(...) custom-call(f32[64,256,256]{2,1,0:T(8,128)S(1)} %get-tuple-element.40.refs_0_, ...), custom_call_target="tpu_custom_call" | custom-call | tf_op jit(solution)/shard_map/results/pallas_call | solution.py:172
where the time goes:
time: 377 us; the launch traced here: 376 us
  Pallas kernels  374 us (99%)
    pallas_call x3, Pallas kernels, call(): pl.pallas_call(kernel, out_shape=[t for t, _ in outs.values()], in_specs=...  374 us

commit v1 on v0

--- a/solution.py
+++ b/solution.py
@@ -43,18 +43,22 @@
 
 def wide(a, b, ca, cb):
     (ah, al), (bh, bl) = a, b
-    if ah.shape[ca] < 512:
-        return dot(jnp.concatenate([ah, ah, al], ca), jnp.concatenate([bh, bl, bh], cb), ((ca,), (cb,)))
     rows = ah.shape[1 - ca]
     both = dot(jnp.concatenate([ah, al], 1 - ca), bh, ((ca,), (cb,)))
     return both[:rows] + both[rows:] + dot(ah, bl, ((ca,), (cb,)))
 
 
+def near(a, b):
+    (ah, al), (bh, bl) = a, b
+    return dot(jnp.concatenate([ah, ah, al, al], 1), jnp.concatenate([bh, bl, bh, bl], 1), ((1,), (1,)))
+
+
 def side(a, b):
     (ah, al), (bh, bl) = a, b
-    width = bh.shape[1]
-    both = dot(ah, jnp.concatenate([bh, bl], 1))
-    return both[:, :width] + both[:, width:] + dot(al, bh)
+    rows, width = ah.shape[0], bh.shape[1]
+    four = dot(jnp.concatenate([ah, al], 0), jnp.concatenate([bh, bl], 1))
+    high, low = four[:rows], four[rows:]
+    return high[:, :width] + (high[:, width:] + low[:, :width] + low[:, width:])
 
 
 def normalized(h):
@@ -191,6 +195,7 @@
         self.real, self.cells = rows * feat, up16(rows * feat)
         self.hd = width // HEADS
         self.scale = self.hd ** (-0.5)
+        self.halves = [queries for queries, _ in blocks(feat, rows)]
 
     def sites(self, r, site, keys_along):
         if site == 1:
@@ -379,9 +384,9 @@
         pl.semaphore_wait(barrier, 1)
 
         def relay(table, half):
-            at = slice(half * self.width // 2, (half + 1) * self.width // 2)
-            src, dst = r.y_v.at[table, 0:real, at], r.got.at[table, :, at]
-            return remote(src, dst, r.send.at[table, half], r.recv.at[table, half], other)
+            at = self.halves[half]
+            at = slice(at.start, min(at.stop, real))
+            return remote(r.y_v.at[table, at], r.got.at[table, at], r.send.at[table, half], r.recv.at[table, half], other)
 
         @pl.loop(0, 2 * t)
         def _(step):
@@ -467,7 +472,7 @@
             def scores(head, queries, keys, bias):
                 q = parts(r.qkv_v, site, queries, lanes(head, hd))
                 k = parts(r.qkv_v, site, keys, lanes(HEADS + head, hd))
-                return wide(q, k, 1, 1)
+                return near(q, k)
 
             def softmax(head, queries, keys, bias, s):
                 s = s + bias[...]
@@ -501,28 +506,30 @@
         def _():
             self.split_mlp(r)
 
-        def up(j):
-            return wide(parts(r.a_v, 2), parts(r.wup_v, slice(None), slice(j * TILE, (j + 1) * TILE)), 1, 0)
-
-        tiles = ff // TILE
-        z = up(0)
-        for j in range(tiles):
-            at = slice(j * TILE, (j + 1) * TILE)
-            following = up(j + 1) if j + 1 < tiles else None
-            g, gp = gelu_parts(z)
-            put(r.g_v, (slice(None), at), g)
-            r.gp_v[:, at] = gp
-            z = following
+        def feed_forward(cells):
+            def up(at):
+                return wide(parts(r.a_v, 2, cells), parts(r.wup_v, slice(None), at), 1, 0)
+
+            def activate(at, z):
+                g, gp = gelu_parts(z)
+                put(r.g_v, (cells, at), g)
+                r.gp_v[cells, at] = gp
+
+            staggered([(slice(j, j + TILE),) for j in range(0, ff, TILE)], up, activate)
+            r.y_v[table, cells] = r.h_v[0, cells] + wide(parts(r.g_v, cells), parts(r.wdown_v), 1, 0)
+
+        @pl.when(section == 0)
+        def _():
+            for half, cells in enumerate(self.halves):
+                feed_forward(cells)
+                relay(table, half).start()
+
+        @pl.when(section == 1)
+        def _():
+            feed_forward(slice(0, c))
+
         keep(r.g_v, r.gs.at[table])
         keep(r.gp_v, r.gps.at[table], True)
-        for half in range(2):
-            at = slice(half * w // 2, (half + 1) * w // 2)
-            r.y_v[table, :, at] = r.h_v[0, :, at] + wide(parts(r.g_v), parts(r.wdown_v, slice(None), at), 1, 0)
-
-            @pl.when(section == 0)
-            def _():
-                relay(table, half).start()
-
         keep(r.y_v.at[table, 0:real], r.out.at[table])
         for copy in stores:
             copy.wait()
@@ -540,6 +547,26 @@
             stores.append(start(src, dst, r.out_sem.at[len(stores)]))
 
         fill_biases(self.feat, self.rows, r.ctx[table], r.col_bias[0], 0)
+
+        def through_norm(site, cells, da):
+            n, k = r.n_v[site, cells], 2 * HEADS + site
+            rstd = r.stat_v[table, cells, k : k + 1]
+            r.small[site : site + 1, :] += jnp.sum(da * n, axis=0, keepdims=True)
+            r.dy_v[cells] += norm_back(n, rstd, r.gains[site], da)
+
+        def mlp_back(cells):
+            put(r.dys_v, (cells,), r.dy_v[cells])
+
+            def down(at):
+                return wide(parts(r.dys_v, cells), parts(r.wdown_v, at), 1, 1)
+
+            def deactivate(at, dg):
+                put(r.g_v, (cells, at), dg * r.gp_v[cells, at])
+
+            staggered([(slice(j, j + TILE),) for j in range(0, ff, TILE)], down, deactivate)
+            through_norm(2, cells, wide(parts(r.g_v, cells), parts(r.wup_v), 1, 1))
+
+        r.dy_v[real:, :] = jnp.zeros((c - real, w), F32)
 
         @pl.when(section == 0)
         def _():
@@ -548,40 +575,21 @@
                 start(r.qkvs.at[table], r.qkv_v, r.in_sem.at[1]),
                 start(r.gps.at[table], r.gp_v, r.in_sem.at[2]),
             ]
-            for half in range(2):
-                relay(table, half).wait()
-            r.dy_v[0:real] = r.got[table]
             for copy in loads:
                 copy.wait()
+            for half, cells in enumerate(self.halves):
+                relay(table, half).wait()
+                came = slice(cells.start, min(cells.stop, real))
+                r.dy_v[came] = r.got[table, came]
+                mlp_back(cells)
 
         @pl.when(section == 1)
         def _():
             pltpu.make_async_copy(r.cot.at[table], r.dy_v.at[0:real], r.in_sem.at[1]).wait()
-
-        r.dy_v[real:, :] = jnp.zeros((c - real, w), F32)
-        put(r.dys_v, (), r.dy_v[...])
+            mlp_back(slice(0, c))
+
         keep(r.dys_v, r.dys.at[table])
-
-        def down(j):
-            return wide(parts(r.dys_v), parts(r.wdown_v, slice(j * TILE, (j + 1) * TILE)), 1, 1)
-
-        tiles = ff // TILE
-        dg = down(0)
-        for j in range(tiles):
-            at = slice(j * TILE, (j + 1) * TILE)
-            following = down(j + 1) if j + 1 < tiles else None
-            put(r.g_v, (slice(None), at), dg * r.gp_v[:, at])
-            dg = following
         keep(r.g_v, r.dzs.at[table])
-        da = wide(parts(r.g_v), parts(r.wup_v), 1, 1)
-
-        def through_norm(site, da):
-            n, k = r.n_v[site], 2 * HEADS + site
-            rstd = r.stat_v[table, :, k : k + 1]
-            r.small[site : site + 1, :] += jnp.sum(da * n, axis=0, keepdims=True)
-            return norm_back(n, rstd, r.gains[site], da)
-
-        r.dy_v[...] += through_norm(2, da)
         for site in (1, 0):
             if site == 0:
                 self.set_out(r, r.dy_v, real)
@@ -595,8 +603,7 @@
 
             def products(head, queries, keys, bias):
                 do = parts(r.do_v, queries, lanes(head, hd))
-                s = wide(part_of(1, head, keys), part_of(0, head, queries), 1, 1)
-                return s, wide(part_of(2, head, keys), do, 1, 1)
+                return near(part_of(1, head, keys), part_of(0, head, queries)), near(part_of(2, head, keys), do)
 
             def gradients(head, queries, keys, bias, state):
                 s, dp = state
@@ -632,7 +639,7 @@
                 put(r.qkv_v, (site, slice(None), at), r.dqkv_f[:, at])
             keep(r.qkv_v.at[:, site], r.dqkvs.at[table, :, site])
             da = wide(parts(r.qkv_v, site), parts(r.win_v, site), 1, 1)
-            r.dy_v[...] += through_norm(site, da)
+            through_norm(site, slice(None), da)
 
         self.set_out(r, r.dy_v, real)
         self.by_features(r, r.dy_v)

time: 377 us -> 435 us (1.15)
  Pallas kernels: 374 us -> 431 us
    pallas_call x3, Pallas kernels: 374 us -> 431 us  [call(): pl.pallas_call(kernel, out_shape=[t for t, _ in outs.values()], in_specs=...]
where the time goes in v1:
time: 435 us; the launch traced here: 433 us
  Pallas kernels  431 us (99%)
    pallas_call x3, Pallas kernels, call(): pl.pallas_call(kernel, out_shape=[t for t, _ in outs.values()], in_specs=...  431 us

profile of v1, /device:TPU:0, one launch (start us, length us, event | category | flops | bytes accessed | tf_op | source)
XLA Modules:
  0.0 433.3 jit_solution(4302135185152800749)
XLA Ops:
  0.6 1.4 copy.18.refs_1_
  2.0 250.6 %layers.1 = (f32[2,456,512]{2,1,0:T(8,128)}, f32[2,456,512]{2,1,0:T(8,128)}, f32[2,3,464,512]{3,2,1,0:T(8,128)}, bf16[2,2,2,464,1536]{4,3,2,1,0:T(8,128)(2,1)}, ...) custom-call(f32[2,456,512]{2,1,0:T(8,128)} %bitcast.32, ...), custom_call_target="tpu_custom_call" | custom-call | tf_op jit(solution)/shard_map/layers/pallas_call | solution.py:176
  252.7 171.5 %weight_gradient_sum.1 = (f32[64,256,256]{2,1,0:T(8,128)S(1)}, f32[8,512]{1,0:T(8,128)}, f32[2,456,512]{2,1,0:T(8,128)S(1)}, f32[2,456,512]{2,1,0:T(8,128)S(1)}) custom-call(bf16[2,2,3,464,512]{4,3,2,1,0:T(8,128)(2,1)} %get-tuple-element.30.refs_0_, bf16[2,2,2,464,512]{4,3,2,1,0:T(8,128)(2,1)} %get-tuple-element.31.refs_1_, ...), custom_call_target="tpu_custom_call" | custom-call | tf_op jit(solution)/shard_map/weight_gradient_sum/pallas_call | solution.py:176
  424.2 8.9 %results.1 = (f32[2,512,1536]{2,1,0:T(8,128)}, f32[2,512,512]{2,1,0:T(8,128)}, f32[512,2048]{1,0:T(8,128)}, f32[2048,512]{1,0:T(8,128)}, f32[2,456,512]{2,1,0:T(...) custom-call(f32[64,256,256]{2,1,0:T(8,128)S(1)} %get-tuple-element.40.refs_0_, ...), custom_call_target="tpu_custom_call" | custom-call | tf_op jit(solution)/shard_map/results/pallas_call | solution.py:176

commit v2 on v0

--- a/solution.py
+++ b/solution.py
@@ -48,6 +48,11 @@
     rows = ah.shape[1 - ca]
     both = dot(jnp.concatenate([ah, al], 1 - ca), bh, ((ca,), (cb,)))
     return both[:rows] + both[rows:] + dot(ah, bl, ((ca,), (cb,)))
+
+
+def near(a, b):
+    (ah, al), (bh, bl) = a, b
+    return dot(jnp.concatenate([ah, ah, al, al], 1), jnp.concatenate([bh, bl, bh, bl], 1), ((1,), (1,)))
 
 
 def side(a, b):
@@ -285,6 +290,8 @@
 
         return call("layers", body, 1, ins, outs, scratch, VMEM_LIMIT)
 
+    attention_pieces = 8
+
     def raw_pieces(self, r):
         w, ff = self.width, self.ff
         half, wide_in, step = w // 2, 3 * w, self.SPLIT_ROWS
@@ -300,7 +307,7 @@
             (r.wout.at[1, top], r.n_v.at[0, top], r.wout_v, (1,), 0, whole, 4),
             (r.wout.at[1, rest], r.spare_v, r.wout_v, (1,), half, whole, 5),
         ]
-        self.attention_pieces = len(pieces)
+        assert len(pieces) == self.attention_pieces
         pieces.append((r.wup.at[top], bigger, r.wup_v, (), 0, whole, 1))
         pieces.append((r.wup.at[rest, 0:wide_in], big, r.wup_v, (), half, slice(0, wide_in), 0))
         pieces.append((r.wup.at[rest, wide_in:ff], r.spare_v, r.wup_v, (), half, slice(wide_in, ff), 5))
@@ -340,16 +347,18 @@
         if later:
             self.raw_copy(r, later[0]).start()
 
-    def start_raw(self, r):
+    def start_raw(self, r, mlp):
         seen = set()
         for i, piece in enumerate(self.raw_pieces(r)):
-            if piece[-1] not in seen:
+            if piece[-1] not in seen and mlp == (i >= self.attention_pieces):
                 self.raw_copy(r, i).start()
             seen.add(piece[-1])
 
     def split_attention(self, r):
+        self.start_raw(r, False)
         for i in range(self.attention_pieces):
             self.split_piece(r, i)
+        self.start_raw(r, True)
 
     def split_mlp(self, r):
         for i in range(self.attention_pieces, len(self.raw_pieces(r))):
@@ -361,7 +370,6 @@
         other = {"section": 1 - section}
         barrier = pltpu.get_barrier_semaphore()
         pl.semaphore_signal(barrier, inc=1, device_id=other, device_id_type=pl.DeviceIdType.MESH)
-        self.start_raw(r)
 
         @pl.when(section == 0)
         def _():
@@ -467,7 +475,7 @@
             def scores(head, queries, keys, bias):
                 q = parts(r.qkv_v, site, queries, lanes(head, hd))
                 k = parts(r.qkv_v, site, keys, lanes(HEADS + head, hd))
-                return wide(q, k, 1, 1)
+                return near(q, k)
 
             def softmax(head, queries, keys, bias, s):
                 s = s + bias[...]
@@ -562,6 +570,8 @@
         put(r.dys_v, (), r.dy_v[...])
         keep(r.dys_v, r.dys.at[table])
 
+        column_tiles = [slice(j, j + 256) for j in range(0, w, 256)]
+
         def down(j):
             return wide(parts(r.dys_v), parts(r.wdown_v, slice(j * TILE, (j + 1) * TILE)), 1, 1)
 
@@ -573,7 +583,7 @@
             put(r.g_v, (slice(None), at), dg * r.gp_v[:, at])
             dg = following
         keep(r.g_v, r.dzs.at[table])
-        da = wide(parts(r.g_v), parts(r.wup_v), 1, 1)
+        da = jnp.concatenate([wide(parts(r.g_v), parts(r.wup_v, at), 1, 1) for at in column_tiles], 1)
 
         def through_norm(site, da):
             n, k = r.n_v[site], 2 * HEADS + site
@@ -595,8 +605,7 @@
 
             def products(head, queries, keys, bias):
                 do = parts(r.do_v, queries, lanes(head, hd))
-                s = wide(part_of(1, head, keys), part_of(0, head, queries), 1, 1)
-                return s, wide(part_of(2, head, keys), do, 1, 1)
+                return near(part_of(1, head, keys), part_of(0, head, queries)), near(part_of(2, head, keys), do)
 
             def gradients(head, queries, keys, bias, state):
                 s, dp = state
@@ -631,7 +640,7 @@
                 at = slice(j * TILE, (j + 1) * TILE)
                 put(r.qkv_v, (site, slice(None), at), r.dqkv_f[:, at])
             keep(r.qkv_v.at[:, site], r.dqkvs.at[table, :, site])
-            da = wide(parts(r.qkv_v, site), parts(r.win_v, site), 1, 1)
+            da = jnp.concatenate([wide(parts(r.qkv_v, site), parts(r.win_v, site, at), 1, 1) for at in column_tiles], 1)
             r.dy_v[...] += through_norm(site, da)
 
         self.set_out(r, r.dy_v, real)

time: 377 us -> 376 us (level)
  no operation moved by 1% of the time
where the time goes in v2:
time: 376 us
  Pallas kernels  373 us (99%)
    pallas_call x3, Pallas kernels, call(): pl.pallas_call(kernel, out_shape=[t for t, _ in outs.values()], in_specs=...  373 us

profile of v2, /device:TPU:0, one launch (start us, length us, event | category | flops | bytes accessed | tf_op | source)
XLA Modules:
  0.0 375.7 jit_solution(6853999347151674009)
XLA Ops:
  0.6 1.4 copy.18.refs_1_
  2.0 195.2 %layers.1 = (f32[2,456,512]{2,1,0:T(8,128)}, f32[2,456,512]{2,1,0:T(8,128)}, f32[2,3,464,512]{3,2,1,0:T(8,128)}, bf16[2,2,2,464,1536]{4,3,2,1,0:T(8,128)(2,1)}, ...) custom-call(f32[2,456,512]{2,1,0:T(8,128)} %bitcast.32, ...), custom_call_target="tpu_custom_call" | custom-call | tf_op jit(solution)/shard_map/layers/pallas_call | solution.py:177
  197.2 169.4 %weight_gradient_sum.1 = (f32[64,256,256]{2,1,0:T(8,128)S(1)}, f32[8,512]{1,0:T(8,128)}, f32[2,456,512]{2,1,0:T(8,128)S(1)}, f32[2,456,512]{2,1,0:T(8,128)S(1)}) custom-call(bf16[2,2,3,464,512]{4,3,2,1,0:T(8,128)(2,1)} %get-tuple-element.30.refs_0_, bf16[2,2,2,464,512]{4,3,2,1,0:T(8,128)(2,1)} %get-tuple-element.31.refs_1_, ...), custom_call_target="tpu_custom_call" | custom-call | tf_op jit(solution)/shard_map/weight_gradient_sum/pallas_call | solution.py:177
  366.6 8.9 %results.1 = (f32[2,512,1536]{2,1,0:T(8,128)}, f32[2,512,512]{2,1,0:T(8,128)}, f32[512,2048]{1,0:T(8,128)}, f32[2048,512]{1,0:T(8,128)}, f32[2,456,512]{2,1,0:T(...) custom-call(f32[64,256,256]{2,1,0:T(8,128)S(1)} %get-tuple-element.40.refs_0_, ...), custom_call_target="tpu_custom_call" | custom-call | tf_op jit(solution)/shard_map/results/pallas_call | solution.py:177

commit v3 on v2

--- a/solution.py
+++ b/solution.py
@@ -196,6 +196,7 @@
         self.real, self.cells = rows * feat, up16(rows * feat)
         self.hd = width // HEADS
         self.scale = self.hd ** (-0.5)
+        self.halves = [queries for queries, _ in blocks(feat, rows)]
 
     def sites(self, r, site, keys_along):
         if site == 1:
@@ -386,9 +387,12 @@
         r.small[...] = jnp.zeros_like(r.small)
         pl.semaphore_wait(barrier, 1)
 
-        def relay(table, half):
-            at = slice(half * self.width // 2, (half + 1) * self.width // 2)
-            src, dst = r.y_v.at[table, 0:real, at], r.got.at[table, :, at]
+        def relay(table, half, back):
+            at = self.halves[half]
+            at = (slice(at.start, min(at.stop, real)),)
+            if not back:
+                at = (slice(0, real), slice(half * self.width // 2, (half + 1) * self.width // 2))
+            src, dst = r.y_v.at[(table, *at)], r.got.at[(table, *at)]
             return remote(src, dst, r.send.at[table, half], r.recv.at[table, half], other)
 
         @pl.loop(0, 2 * t)
@@ -408,7 +412,7 @@
         def _():
             for table in range(t):
                 for half in range(2):
-                    relay(table, half).wait_send()
+                    relay(table, half, True).wait_send()
 
     def forward(self, r, table, section, relay, step):
         c, w, ff, hd, real = self.cells, self.width, self.ff, self.hd, self.real
@@ -453,7 +457,7 @@
         def _():
             start(r.cot.at[table], r.dy_v.at[0:real], r.in_sem.at[1])
             for half in range(2):
-                relay(table, half).wait_recv()
+                relay(table, half, False).wait_recv()
             self.set_out(r, r.got.at[table], real)
 
         self.by_rows(r, r.h_v.at[0])
@@ -529,7 +533,7 @@
 
             @pl.when(section == 0)
             def _():
-                relay(table, half).start()
+                relay(table, half, False).start()
 
         keep(r.y_v.at[table, 0:real], r.out.at[table])
         for copy in stores:
@@ -548,6 +552,29 @@
             stores.append(start(src, dst, r.out_sem.at[len(stores)]))
 
         fill_biases(self.feat, self.rows, r.ctx[table], r.col_bias[0], 0)
+
+        column_tiles = [slice(j, j + 256) for j in range(0, w, 256)]
+
+        def through_norm(site, cells, da):
+            n, k = r.n_v[site, cells], 2 * HEADS + site
+            rstd = r.stat_v[table, cells, k : k + 1]
+            r.small[site : site + 1, :] += jnp.sum(da * n, axis=0, keepdims=True)
+            r.dy_v[cells] += norm_back(n, rstd, r.gains[site], da)
+
+        def mlp_back(cells):
+            put(r.dys_v, (cells,), r.dy_v[cells])
+
+            def down(at):
+                return wide(parts(r.dys_v, cells), parts(r.wdown_v, at), 1, 1)
+
+            def deactivate(at, dg):
+                put(r.g_v, (cells, at), dg * r.gp_v[cells, at])
+
+            staggered([(slice(j, j + TILE),) for j in range(0, ff, TILE)], down, deactivate)
+            da = [wide(parts(r.g_v, cells), parts(r.wup_v, at), 1, 1) for at in column_tiles]
+            through_norm(2, cells, jnp.concatenate(da, 1))
+
+        r.dy_v[real:, :] = jnp.zeros((c - real, w), F32)
 
         @pl.when(section == 0)
         def _():
@@ -557,41 +584,22 @@
                 start(r.gps.at[table], r.gp_v, r.in_sem.at[2]),
             ]
             for half in range(2):
-                relay(table, half).wait()
-            r.dy_v[0:real] = r.got[table]
+                relay(table, half, False).wait_send()
             for copy in loads:
                 copy.wait()
+            for half, cells in enumerate(self.halves):
+                relay(table, half, True).wait_recv()
+                came = slice(cells.start, min(cells.stop, real))
+                r.dy_v[came] = r.got[table, came]
+                mlp_back(cells)
 
         @pl.when(section == 1)
         def _():
             pltpu.make_async_copy(r.cot.at[table], r.dy_v.at[0:real], r.in_sem.at[1]).wait()
-
-        r.dy_v[real:, :] = jnp.zeros((c - real, w), F32)
-        put(r.dys_v, (), r.dy_v[...])
+            mlp_back(slice(0, c))
+
         keep(r.dys_v, r.dys.at[table])
-
-        column_tiles = [slice(j, j + 256) for j in range(0, w, 256)]
-
-        def down(j):
-            return wide(parts(r.dys_v), parts(r.wdown_v, slice(j * TILE, (j + 1) * TILE)), 1, 1)
-
-        tiles = ff // TILE
-        dg = down(0)
-        for j in range(tiles):
-            at = slice(j * TILE, (j + 1) * TILE)
-            following = down(j + 1) if j + 1 < tiles else None
-            put(r.g_v, (slice(None), at), dg * r.gp_v[:, at])
-            dg = following
         keep(r.g_v, r.dzs.at[table])
-        da = jnp.concatenate([wide(parts(r.g_v), parts(r.wup_v, at), 1, 1) for at in column_tiles], 1)
-
-        def through_norm(site, da):
-            n, k = r.n_v[site], 2 * HEADS + site
-            rstd = r.stat_v[table, :, k : k + 1]
-            r.small[site : site + 1, :] += jnp.sum(da * n, axis=0, keepdims=True)
-            return norm_back(n, rstd, r.gains[site], da)
-
-        r.dy_v[...] += through_norm(2, da)
         for site in (1, 0):
             if site == 0:
                 self.set_out(r, r.dy_v, real)
@@ -641,7 +649,7 @@
                 put(r.qkv_v, (site, slice(None), at), r.dqkv_f[:, at])
             keep(r.qkv_v.at[:, site], r.dqkvs.at[table, :, site])
             da = jnp.concatenate([wide(parts(r.qkv_v, site), parts(r.win_v, site, at), 1, 1) for at in column_tiles], 1)
-            r.dy_v[...] += through_norm(site, da)
+            through_norm(site, slice(None), da)
 
         self.set_out(r, r.dy_v, real)
         self.by_features(r, r.dy_v)
@@ -658,7 +666,7 @@
         def _():
             r.y_v[table] = r.dy_v[...]
             for half in range(2):
-                relay(table, half).start()
+                relay(table, half, True).start()
 
         keep(r.y_v.at[table, 0:real], r.din.at[table])
         for copy in stores:

time: 376 us -> 449 us (1.19)
  Pallas kernels: 373 us -> 445 us
    pallas_call x3, Pallas kernels: 373 us -> 445 us  [call(): pl.pallas_call(kernel, out_shape=[t for t, _ in outs.values()], in_specs=...]
where the time goes in v3:
time: 449 us; the launch traced here: 447 us
  Pallas kernels  445 us (99%)
    pallas_call x3, Pallas kernels, call(): pl.pallas_call(kernel, out_shape=[t for t, _ in outs.values()], in_specs=...  445 us

profile of v3, /device:TPU:0, one launch (start us, length us, event | category | flops | bytes accessed | tf_op | source)
XLA Modules:
  0.0 446.9 jit_solution(15957462233706321838)
XLA Ops:
  0.6 1.4 copy.18.refs_1_
  2.0 266.8 %layers.1 = (f32[2,456,512]{2,1,0:T(8,128)}, f32[2,456,512]{2,1,0:T(8,128)}, f32[2,3,464,512]{3,2,1,0:T(8,128)}, bf16[2,2,2,464,1536]{4,3,2,1,0:T(8,128)(2,1)}, ...) custom-call(f32[2,456,512]{2,1,0:T(8,128)} %bitcast.32, ...), custom_call_target="tpu_custom_call" | custom-call | tf_op jit(solution)/shard_map/layers/pallas_call | solution.py:177
  268.9 168.9 %weight_gradient_sum.1 = (f32[64,256,256]{2,1,0:T(8,128)S(1)}, f32[8,512]{1,0:T(8,128)}, f32[2,456,512]{2,1,0:T(8,128)S(1)}, f32[2,456,512]{2,1,0:T(8,128)S(1)}) custom-call(bf16[2,2,3,464,512]{4,3,2,1,0:T(8,128)(2,1)} %get-tuple-element.30.refs_0_, bf16[2,2,2,464,512]{4,3,2,1,0:T(8,128)(2,1)} %get-tuple-element.31.refs_1_, ...), custom_call_target="tpu_custom_call" | custom-call | tf_op jit(solution)/shard_map/weight_gradient_sum/pallas_call | solution.py:177
  437.8 8.9 %results.1 = (f32[2,512,1536]{2,1,0:T(8,128)}, f32[2,512,512]{2,1,0:T(8,128)}, f32[512,2048]{1,0:T(8,128)}, f32[2048,512]{1,0:T(8,128)}, f32[2,456,512]{2,1,0:T(...) custom-call(f32[64,256,256]{2,1,0:T(8,128)S(1)} %get-tuple-element.40.refs_0_, ...), custom_call_target="tpu_custom_call" | custom-call | tf_op jit(solution)/shard_map/results/pallas_call | solution.py:177
